TPU v7x, 32 devices: a whole 2x2x4 slice. The times are simulated.
32 devices in a mesh: group: 8 (over y, x, core), replica: 4 (over z).
Axes of the slice: x: 2, y: 2, z: 4, core: 2. Of those that a mesh axis runs over, the one named last changes fastest.
Arguments:
- tokens: bfloat16 [4, 1024, 960], P('replica', 'group'), may hold values from -6 to 6
- positions: int32 [4, 1024], P('replica', 'group'), may hold values from 0 to 999, as said below
- gain_attn: bfloat16 [2, 960], P(None, 'group'), may hold values from 0.5 to 1.5
- w_query: bfloat16 [2, 960, 960], P(None, 'group'), may hold values from -0.1875 to 0.1875
- w_key: bfloat16 [2, 960, 320], P(None, 'group'), may hold values from -0.1875 to 0.1875
- w_value: bfloat16 [2, 960, 320], P(None, 'group'), may hold values from -0.1875 to 0.1875
- w_out: bfloat16 [2, 960, 960], P(None, 'group'), may hold values from -0.5 to 0.5
- gain_ffn: bfloat16 [2, 960], P(None, 'group'), may hold values from 0.5 to 1.5
- w_gate: bfloat16 [2, 960, 2560], P(None, 'group'), may hold values from -0.1875 to 0.1875
- w_up: bfloat16 [2, 960, 2560], P(None, 'group'), may hold values from -0.1875 to 0.1875
- w_down: bfloat16 [2, 2560, 960], P(None, 'group'), may hold values from -0.125 to 0.125
- cotangent: bfloat16 [4, 1024, 960], P('replica', 'group'), may hold values from -6 to 6
Outputs:
- activations: float32 [4, 2, 1024, 960], P('replica', None, 'group')
- grad_tokens: float32 [4, 1024, 960], P('replica', 'group')
- grad_gain_attn: float32 [2, 960], P(None, 'group')
- grad_w_query: float32 [2, 960, 960], P(None, 'group')
- grad_w_key: float32 [2, 960, 320], P(None, 'group')
- grad_w_value: float32 [2, 960, 320], P(None, 'group')
- grad_w_out: float32 [2, 960, 960], P(None, 'group')
- grad_gain_ffn: float32 [2, 960], P(None, 'group')
- grad_w_gate: float32 [2, 960, 2560], P(None, 'group')
- grad_w_up: float32 [2, 960, 2560], P(None, 'group')
- grad_w_down: float32 [2, 2560, 960], P(None, 'group')
Inputs may be any that keep to these rules, and one draw needn't show every extreme that they name: In each sequence positions are 0 at a document's first token and rise by one per token inside a document; every document except a sequence's last has 100 to 1000 tokens; the first token of every sequence has position 0.
All inputs are finite; a program needn't handle non-finite values.
Results may differ from a plain program's by a relative error of at most 0.02.
Values may be sent and summed in bfloat16 or wider, within the bound.
A program may use at most 320 MiB of HBM per device.

v0:
```python
import jax
import jax.numpy as jnp
from jax import lax
from jax.sharding import PartitionSpec as P

HEADS = 15
KV_HEADS = 5
HEAD_DIM = 64
LAYERS = 2
epsilon = 1e-05
rope_base = 100000.0


def forward_dot(left, right):
    return jnp.dot(left, right, preferred_element_type=jnp.float32)


def over_rows(left, right):
    return lax.dot_general(
        left, right, (((0,), (0,)), ((), ())), preferred_element_type=jnp.float32
    )


def against(left, right):
    return lax.dot_general(
        left, right, (((1,), (1,)), ((), ())), preferred_element_type=jnp.float32
    )


def rope_tables(token_positions):
    half_dim = HEAD_DIM // 2
    frequency = rope_base ** (-2.0 * jnp.arange(half_dim, dtype=jnp.float32) / HEAD_DIM)
    angles = token_positions.astype(jnp.float32)[:, None] * frequency[None, :]
    return (jnp.cos(angles)[:, None, :], jnp.sin(angles)[:, None, :])


def rotate(vectors, cosine, sine_table):
    half_dim = HEAD_DIM // 2
    leading, trailing = (vectors[..., :half_dim], vectors[..., half_dim:])
    return jnp.concatenate(
        [leading * cosine - trailing * sine_table, trailing * cosine + leading * sine_table],
        axis=-1,
    )


def rotate_back(vectors, cosine, sine_table):
    half_dim = HEAD_DIM // 2
    leading, trailing = (vectors[..., :half_dim], vectors[..., half_dim:])
    return jnp.concatenate(
        [leading * cosine + trailing * sine_table, trailing * cosine - leading * sine_table],
        axis=-1,
    )


def norm_forward(stream):
    inverse = lax.rsqrt(jnp.mean(stream * stream, axis=-1, keepdims=True) + epsilon)
    return (inverse, stream * inverse)


def norm_back(grad_unit, unit_value, inverse):
    return inverse * (
        grad_unit - unit_value * jnp.mean(grad_unit * unit_value, axis=-1, keepdims=True)
    )


def masked_scores(grouped, key_all, allowed):
    scores = (
        jnp.einsum("qkgd,skd->kgqs", grouped, key_all, preferred_element_type=jnp.float32) * 0.125
    )
    return jnp.where(allowed[None, None], scores, -1e30)


def layer_forward(stream, gathered, allowed, cosine, sine_table):
    gain_attn, w_query, w_key, w_value, w_out, gain_ffn, w_gate, w_up, w_down = gathered
    row_count = stream.shape[0]
    inverse_attn, unit_attn = norm_forward(stream)
    normed_attn = (unit_attn * gain_attn.astype(jnp.float32)).astype(jnp.bfloat16)
    queries = rotate(
        forward_dot(normed_attn, w_query).reshape(row_count, HEADS, HEAD_DIM), cosine, sine_table
    ).astype(jnp.bfloat16)
    own_keys = rotate(
        forward_dot(normed_attn, w_key).reshape(row_count, KV_HEADS, HEAD_DIM), cosine, sine_table
    ).astype(jnp.bfloat16)
    own_values = (
        forward_dot(normed_attn, w_value)
        .astype(jnp.bfloat16)
        .reshape(row_count, KV_HEADS, HEAD_DIM)
    )
    key_all, value_all = (
        lax.all_gather(own_keys, "group", axis=0, tiled=True),
        lax.all_gather(own_values, "group", axis=0, tiled=True),
    )
    grouped = queries.reshape(row_count, KV_HEADS, HEADS // KV_HEADS, HEAD_DIM)
    scores = masked_scores(grouped, key_all, allowed)
    row_max = jnp.max(scores, axis=-1, keepdims=True)
    exponent = jnp.exp(scores - row_max)
    row_total = jnp.sum(exponent, axis=-1, keepdims=True)
    weights_low = (exponent / row_total).astype(jnp.bfloat16)
    mixed_heads = jnp.einsum(
        "kgqs,skd->qkgd", weights_low, value_all, preferred_element_type=jnp.float32
    )
    mixed_heads = mixed_heads.reshape(row_count, HEADS * HEAD_DIM).astype(jnp.bfloat16)
    after_attn = stream + forward_dot(mixed_heads, w_out)
    inverse_ffn, unit_ffn = norm_forward(after_attn)
    normed_ffn = (unit_ffn * gain_ffn.astype(jnp.float32)).astype(jnp.bfloat16)
    gate_value = forward_dot(normed_ffn, w_gate)
    up_value = forward_dot(normed_ffn, w_up)
    hidden = (jax.nn.silu(gate_value) * up_value).astype(jnp.bfloat16)
    result = after_attn + forward_dot(hidden, w_down)
    saved = (
        unit_attn,
        inverse_attn,
        normed_attn,
        grouped,
        row_max,
        row_total,
        mixed_heads,
        unit_ffn,
        inverse_ffn,
        normed_ffn,
        gate_value,
        up_value,
        hidden,
    )
    return (result, saved, (own_keys, own_values), (key_all, value_all))


def replica_total(shares):
    (
        share_gain_attn,
        share_query,
        share_key,
        share_value,
        share_out,
        share_gain_ffn,
        share_gate,
        share_up,
        share_down,
    ) = shares
    return lax.psum(
        (
            share_gain_attn,
            share_query,
            share_key,
            share_value,
            share_out,
            share_gain_ffn,
            share_gate,
            share_up,
            share_down,
        ),
        "replica",
    )


def owned_columns(matrix, owner, members):
    width = matrix.shape[1] // members
    return lax.dynamic_slice_in_dim(matrix, owner * width, width, 1)


def layer_backward(grad_result, gathered, saved, key_all, value_all, allowed, cosine, sine_table):
    gain_attn, w_query, w_key, w_value, w_out, gain_ffn, w_gate, w_up, w_down = gathered
    (
        unit_attn,
        inverse_attn,
        normed_attn,
        grouped,
        row_max,
        row_total,
        mixed_heads,
        unit_ffn,
        inverse_ffn,
        normed_ffn,
        gate_value,
        up_value,
        hidden,
    ) = saved
    row_count = grad_result.shape[0]
    branch_low = grad_result.astype(jnp.bfloat16)
    grad_hidden = against(branch_low, w_down)
    sigmoid_gate = jax.nn.sigmoid(gate_value)
    grad_up_low = (grad_hidden * gate_value * sigmoid_gate).astype(jnp.bfloat16)
    grad_gate_low = (
        grad_hidden * up_value * sigmoid_gate * (1.0 + gate_value * (1.0 - sigmoid_gate))
    ).astype(jnp.bfloat16)
    grad_normed_ffn = against(grad_gate_low, w_gate) + against(grad_up_low, w_up)
    grad_gain_ffn = jnp.sum(grad_normed_ffn * unit_ffn, axis=0)
    grad_after = grad_result + norm_back(
        grad_normed_ffn * gain_ffn.astype(jnp.float32), unit_ffn, inverse_ffn
    )
    after_low = grad_after.astype(jnp.bfloat16)
    grad_mixed = (
        against(after_low, w_out)
        .astype(jnp.bfloat16)
        .reshape(row_count, KV_HEADS, HEADS // KV_HEADS, HEAD_DIM)
    )
    scores = masked_scores(grouped, key_all, allowed)
    weights_soft = jnp.exp(scores - row_max) / row_total
    grad_weights = jnp.einsum(
        "qkgd,skd->kgqs", grad_mixed, value_all, preferred_element_type=jnp.float32
    )
    grad_value_all = jnp.einsum(
        "kgqs,qkgd->skd",
        weights_soft.astype(jnp.bfloat16),
        grad_mixed,
        preferred_element_type=jnp.float32,
    )
    grad_scores = (
        weights_soft * (grad_weights - jnp.sum(grad_weights * weights_soft, axis=-1, keepdims=True))
    ).astype(jnp.bfloat16)
    grad_queries = (
        jnp.einsum("kgqs,skd->qkgd", grad_scores, key_all, preferred_element_type=jnp.float32)
        * 0.125
    )
    grad_key_all = (
        jnp.einsum("kgqs,qkgd->skd", grad_scores, grouped, preferred_element_type=jnp.float32)
        * 0.125
    )
    grad_keys, grad_values = (
        lax.psum_scatter(grad_key_all, "group", scatter_dimension=0, tiled=True),
        lax.psum_scatter(grad_value_all, "group", scatter_dimension=0, tiled=True),
    )
    query_back = rotate_back(grad_queries.reshape(row_count, HEADS, HEAD_DIM), cosine, sine_table)
    query_back = query_back.reshape(row_count, HEADS * HEAD_DIM).astype(jnp.bfloat16)
    key_back = (
        rotate_back(grad_keys, cosine, sine_table)
        .reshape(row_count, KV_HEADS * HEAD_DIM)
        .astype(jnp.bfloat16)
    )
    value_back = grad_values.reshape(row_count, KV_HEADS * HEAD_DIM).astype(jnp.bfloat16)
    grad_normed_attn = (
        against(query_back, w_query) + against(key_back, w_key) + against(value_back, w_value)
    )
    grad_gain_attn = jnp.sum(grad_normed_attn * unit_attn, axis=0)
    grad_stream = grad_after + norm_back(
        grad_normed_attn * gain_attn.astype(jnp.float32), unit_attn, inverse_attn
    )
    owner = lax.axis_index("group")
    members = lax.axis_size("group")
    piece_attn = lax.all_gather(normed_attn, "group", axis=0, tiled=True)
    piece_query = lax.all_gather(query_back, "group", axis=0, tiled=True)
    piece_key = lax.all_gather(key_back, "group", axis=0, tiled=True)
    piece_value = lax.all_gather(value_back, "group", axis=0, tiled=True)
    piece_mixed = lax.all_gather(mixed_heads, "group", axis=0, tiled=True)
    piece_after = lax.all_gather(after_low, "group", axis=0, tiled=True)
    piece_ffn = lax.all_gather(normed_ffn, "group", axis=0, tiled=True)
    piece_gate = lax.all_gather(grad_gate_low, "group", axis=0, tiled=True)
    piece_up = lax.all_gather(grad_up_low, "group", axis=0, tiled=True)
    piece_hidden = lax.all_gather(hidden, "group", axis=0, tiled=True)
    piece_branch = lax.all_gather(branch_low, "group", axis=0, tiled=True)
    left_attn = owned_columns(piece_attn, owner, members)
    left_mixed = owned_columns(piece_mixed, owner, members)
    left_ffn = owned_columns(piece_ffn, owner, members)
    left_hidden = owned_columns(piece_hidden, owner, members)
    gain_shares = (
        lax.psum_scatter(grad_gain_attn, "group", scatter_dimension=0, tiled=True),
        lax.psum_scatter(grad_gain_ffn, "group", scatter_dimension=0, tiled=True),
    )
    shares = (
        gain_shares[0],
        over_rows(left_attn, piece_query),
        over_rows(left_attn, piece_key),
        over_rows(left_attn, piece_value),
        over_rows(left_mixed, piece_after),
        gain_shares[1],
        over_rows(left_ffn, piece_gate),
        over_rows(left_ffn, piece_up),
        over_rows(left_hidden, piece_branch),
    )
    return (grad_stream, shares)


def on_device(
    tokens,
    positions,
    gain_attn,
    w_query,
    w_key,
    w_value,
    w_out,
    gain_ffn,
    w_gate,
    w_up,
    w_down,
    cotangent,
):
    row_count = tokens.shape[1]
    length_all = row_count * lax.axis_size("group")
    row_index = lax.axis_index("group") * row_count + jnp.arange(row_count, dtype=jnp.int32)
    token_positions = positions[0]
    key_index = jnp.arange(length_all, dtype=jnp.int32)
    allowed = (key_index[None, :] <= row_index[:, None]) & (
        key_index[None, :] >= (row_index - token_positions)[:, None]
    )
    cosine, sine_table = rope_tables(token_positions)
    stream = tokens[0].astype(jnp.float32)
    saved_all = []
    own_all = []
    full_all = []
    gathered_all = []
    outputs = []
    for layer_index in range(LAYERS):
        gathered = (
            lax.all_gather(gain_attn[layer_index], "group", axis=0, tiled=True),
            lax.all_gather(w_query[layer_index], "group", axis=0, tiled=True),
            lax.all_gather(w_key[layer_index], "group", axis=0, tiled=True),
            lax.all_gather(w_value[layer_index], "group", axis=0, tiled=True),
            lax.all_gather(w_out[layer_index], "group", axis=0, tiled=True),
            lax.all_gather(gain_ffn[layer_index], "group", axis=0, tiled=True),
            lax.all_gather(w_gate[layer_index], "group", axis=0, tiled=True),
            lax.all_gather(w_up[layer_index], "group", axis=0, tiled=True),
            lax.all_gather(w_down[layer_index], "group", axis=0, tiled=True),
        )
        stream, saved, own_pair, full_pair = layer_forward(
            stream, gathered, allowed, cosine, sine_table
        )
        saved_all.append(saved)
        own_all.append(own_pair)
        full_all.append(full_pair)
        gathered_all.append(gathered)
        outputs.append(stream)
    grad_stream = cotangent[0].astype(jnp.float32)
    owned = [None] * LAYERS
    for layer_index in reversed(range(LAYERS)):
        gathered = (
            lax.all_gather(gain_attn[layer_index], "group", axis=0, tiled=True),
            lax.all_gather(w_query[layer_index], "group", axis=0, tiled=True),
            lax.all_gather(w_key[layer_index], "group", axis=0, tiled=True),
            lax.all_gather(w_value[layer_index], "group", axis=0, tiled=True),
            lax.all_gather(w_out[layer_index], "group", axis=0, tiled=True),
            lax.all_gather(gain_ffn[layer_index], "group", axis=0, tiled=True),
            lax.all_gather(w_gate[layer_index], "group", axis=0, tiled=True),
            lax.all_gather(w_up[layer_index], "group", axis=0, tiled=True),
            lax.all_gather(w_down[layer_index], "group", axis=0, tiled=True),
        )
        key_all, value_all = (
            lax.all_gather(own_all[layer_index][0], "group", axis=0, tiled=True),
            lax.all_gather(own_all[layer_index][1], "group", axis=0, tiled=True),
        )
        grad_stream, shares = layer_backward(
            grad_stream,
            gathered,
            saved_all[layer_index],
            key_all,
            value_all,
            allowed,
            cosine,
            sine_table,
        )
        owned[layer_index] = replica_total(shares)
    stacked = tuple(
        (
            jnp.stack([owned[layer_index][member] for layer_index in range(LAYERS)])
            for member in range(9)
        )
    )
    activations = jnp.stack(outputs)[None]
    return (
        activations,
        grad_stream[None],
        stacked[0],
        stacked[1],
        stacked[2],
        stacked[3],
        stacked[4],
        stacked[5],
        stacked[6],
        stacked[7],
        stacked[8],
    )


def solution(mesh):
    in_specs = (
        P("replica", "group", None),
        P("replica", "group"),
        P(None, "group"),
        P(None, "group", None),
        P(None, "group", None),
        P(None, "group", None),
        P(None, "group", None),
        P(None, "group"),
        P(None, "group", None),
        P(None, "group", None),
        P(None, "group", None),
        P("replica", "group", None),
    )
    out_specs = (
        P("replica", None, "group", None),
        P("replica", "group", None),
        P(None, "group"),
        P(None, "group", None),
        P(None, "group", None),
        P(None, "group", None),
        P(None, "group", None),
        P(None, "group"),
        P(None, "group", None),
        P(None, "group", None),
        P(None, "group", None),
    )
    return jax.shard_map(
        on_device, mesh=mesh, in_specs=in_specs, out_specs=out_specs, check_vma=False
    )
```

profile of v0, /device:TPU:0, one launch (start us, length us, event | category | flops | bytes accessed | tf_op | source)
XLA Modules:
  0.0 1593.5 jit_solution(1129092299961670674)
XLA Ops:
  21.1 15.6 all-reduce.11
  37.8 12.0 all-gather.2
  53.1 10.6 all_gather.158
  64.5 13.1 all-gather.1
  80.3 13.3 all_gather.156
  95.9 20.1 %all-gather.11 = bf16[1,960,320]{2,0,1:T(2,128)(2,1)S(1)} all-gather(bf16[1,120,320]{2,0,1:T(2,128)(2,1)S(1)} %copy.82), channel_id=13, replica_groups=mesh['group'=8,'replica'=4] {'group'}, dimensions={1}, use_global_device_ids=true | all-gather | bytes 691200 | tf_op jit(solution)/shard_map/all_gather | solution.py:306
  119.7 12.5 all-gather.10
  142.8 5.8 fusion.236
  155.5 4.4 fusion.32
  161.8 4.8 multiply_convert_fusion.5
  166.6 38.7 %all-gather.90.cloned.1.call-done = bf16[1,2560,960]{2,1,0:T(8,128)(2,1)} async-done(((bf16[1,320,960]{2,1,0:T(8,128)(2,1)}), bf16[1,2560,960]{2,1,0:T(8,128)(2,1)}) %all-gather.90.cloned.1.call-update) | async-done | bytes 4915216 | tf_op jit(solution)/shard_map/all_gather | solution.py:312
  211.4 12.2 all_gather.169
  224.0 14.7 all_gather.167
  241.4 6.9 fusion.241
  252.6 16.1 %all-gather.94.cloned.1.call-done = bf16[1,960,960]{2,1,0:T(8,128)(2,1)} async-done(((bf16[1,120,960]{2,1,0:T(8,128)(2,1)}), bf16[1,960,960]{2,1,0:T(8,128)(2,1)}) %all-gather.94.cloned.1.call-update) | async-done | bytes 1843216 | tf_op jit(solution)/shard_map/all_gather | solution.py:308
  271.7 39.3 %all-gather.98.cloned.1.call-done = bf16[1,960,2560]{2,1,0:T(8,128)(2,1)} async-done(((bf16[1,120,2560]{2,1,0:T(8,128)(2,1)}), bf16[1,960,2560]{2,1,0:T(8,128)(2,1)}) %all-gather.98.cloned.1.call-update) | async-done | bytes 4915216 | tf_op jit(solution)/shard_map/all_gather | solution.py:311
  311.0 4.3 fusion.20
  315.3 39.3 %all-gather.100.cloned.1.call-done = bf16[1,2560,960]{2,1,0:T(8,128)(2,1)} async-done(((bf16[1,320,960]{2,1,0:T(8,128)(2,1)}), bf16[1,2560,960]{2,1,0:T(8,128)(2,1)}) %all-gather.100.cloned.1.call-update) | async-done | bytes 4915216 | tf_op jit(solution)/shard_map/all_gather | solution.py:312
  354.6 5.4 fusion.10
  360.0 36.1 %all-gather.96.cloned.1.call-done = bf16[1,960,2560]{2,1,0:T(8,128)(2,1)} async-done(((bf16[1,120,2560]{2,1,0:T(8,128)(2,1)}), bf16[1,960,2560]{2,1,0:T(8,128)(2,1)}) %all-gather.96.cloned.1.call-update) | async-done | bytes 4915216 | tf_op jit(solution)/shard_map/all_gather | solution.py:310
  396.1 5.8 multiply_convert_fusion.3
  401.9 4.8 fusion.18
  406.7 4.8 multiply_reduce_fusion
  415.0 7.7 fusion.5
  422.7 6.9 fusion.7
  434.1 5.7 fusion.71
  446.0 25.5 %reduce-scatter.5.cloned.1.call-done = f32[128,5,64]{0,2,1:T(8,128)} async-done(((f32[1024,5,64]{0,2,1:T(8,128)}), f32[128,5,64]{0,2,1:T(8,128)}) %reduce-scatter.5.cloned.1.call-update) | async-done | bytes 163856 | tf_op jit(solution)/shard_map/reduce_scatter | solution.py:220
  474.8 37.7 %reduce-scatter.7.cloned.1.call-done = f32[128,5,64]{0,2,1:T(8,128)} async-done(((f32[1024,5,64]{0,2,1:T(8,128)}), f32[128,5,64]{0,2,1:T(8,128)}) %reduce-scatter.7.cloned.1.call-update) | async-done | bytes 163856 | tf_op jit(solution)/shard_map/reduce_scatter | solution.py:221
  519.0 6.5 multiply_convert_fusion.1
  525.5 5.0 fusion.26
  530.5 4.9 multiply_reduce_fusion.1
  538.8 5.9 fusion.68
  544.7 7.7 fusion.2
  552.4 6.8 fusion.4
  576.6 11.5 all_gather.181
  588.1 12.7 all_gather.183
  608.2 25.1 %all-gather.60.cloned.1.call-done = bf16[1024,960]{0,1:T(8,128)(2,1)} async-done(((bf16[128,960]{0,1:T(8,128)(2,1)}), bf16[1024,960]{0,1:T(8,128)(2,1)}) %all-gather.60.cloned.1.call-update) | async-done | bytes 1966096 | tf_op jit(solution)/shard_map/all_gather | solution.py:244
  636.5 37.8 %reduce-scatter.11.cloned.1.call-done = f32[128,5,64]{0,2,1:T(8,128)} async-done(((f32[1024,5,64]{0,2,1:T(8,128)}), f32[128,5,64]{0,2,1:T(8,128)}) %reduce-scatter.11.cloned.1.call-update) | async-done | bytes 163856 | tf_op jit(solution)/shard_map/reduce_scatter | solution.py:221
  675.2 40.1 %reduce-scatter.9.cloned.1.call-done = f32[128,5,64]{0,2,1:T(8,128)} async-done(((f32[1024,5,64]{0,2,1:T(8,128)}), f32[128,5,64]{0,2,1:T(8,128)}) %reduce-scatter.9.cloned.1.call-update) | async-done | bytes 163856 | tf_op jit(solution)/shard_map/reduce_scatter | solution.py:220
  716.3 11.2 all_gather.180
  727.5 9.6 all_gather.182
  737.1 7.8 all-gather.48.cloned.1.call-done
  749.0 25.8 %all-gather.50.cloned.1.call-done = bf16[1024,960]{0,1:T(8,128)(2,1)} async-done(((bf16[128,960]{0,1:T(8,128)(2,1)}), bf16[1024,960]{0,1:T(8,128)(2,1)}) %all-gather.50.cloned.1.call-update) | async-done | bytes 1966096 | tf_op jit(solution)/shard_map/all_gather | solution.py:241
  778.0 26.3 %all-gather.56.cloned.1.call-done = bf16[1024,960]{0,1:T(8,128)(2,1)} async-done(((bf16[128,960]{0,1:T(8,128)(2,1)}), bf16[1024,960]{0,1:T(8,128)(2,1)}) %all-gather.56.cloned.1.call-update) | async-done | bytes 1966096 | tf_op jit(solution)/shard_map/all_gather | solution.py:244
  804.3 30.1 %all-gather.58.cloned.1.call-done = bf16[1024,960]{0,1:T(8,128)(2,1)} async-done(((bf16[128,960]{0,1:T(8,128)(2,1)}), bf16[1024,960]{0,1:T(8,128)(2,1)}) %all-gather.58.cloned.1.call-update) | async-done | bytes 1966096 | tf_op jit(solution)/shard_map/all_gather | solution.py:245
  837.7 26.2 %all-gather.78.cloned.1.call-done = bf16[1024,960]{0,1:T(8,128)(2,1)} async-done(((bf16[128,960]{0,1:T(8,128)(2,1)}), bf16[1024,960]{0,1:T(8,128)(2,1)}) %all-gather.78.cloned.1.call-update) | async-done | bytes 1966096 | tf_op jit(solution)/shard_map/all_gather | solution.py:250
  864.0 42.9 %all-gather.76.cloned.1.call-done = bf16[1024,2560]{1,0:T(8,128)(2,1)} async-done(((bf16[128,2560]{1,0:T(8,128)(2,1)}), bf16[1024,2560]{1,0:T(8,128)(2,1)}) %all-gather.76.cloned.1.call-update) | async-done | bytes 5242896 | tf_op jit(solution)/shard_map/all_gather | solution.py:249
  906.8 4.3 convolution_bitcast_fusion.6
  911.2 25.2 %all-gather.102.cloned.1.call-done = bf16[1,1024,960]{1,2,0:T(8,128)(2,1)} async-done(((bf16[1,128,960]{1,2,0:T(8,128)(2,1)}), bf16[1,1024,960]{1,2,0:T(8,128)(2,1)}) %all-gather.102.cloned.1.call-update) | async-done | bytes 1966096 | tf_op jit(solution)/shard_map/all_gather | solution.py:250
  936.4 43.5 %all-gather.80.cloned.1.call-done = bf16[1024,2560]{1,0:T(8,128)(2,1)} async-done(((bf16[128,2560]{1,0:T(8,128)(2,1)}), bf16[1024,2560]{1,0:T(8,128)(2,1)}) %all-gather.80.cloned.1.call-update) | async-done | bytes 5242896 | tf_op jit(solution)/shard_map/all_gather | solution.py:249
  979.8 4.3 fusion.78
  984.2 25.1 %all-gather.68.cloned.1.call-done = bf16[1024,960]{0,1:T(8,128)(2,1)} async-done(((bf16[128,960]{0,1:T(8,128)(2,1)}), bf16[1024,960]{0,1:T(8,128)(2,1)}) %all-gather.68.cloned.1.call-update) | async-done | bytes 1966096 | tf_op jit(solution)/shard_map/all_gather | solution.py:246
  1009.2 43.6 %all-gather.74.cloned.1.call-done = bf16[1024,2560]{1,0:T(8,128)(2,1)} async-done(((bf16[128,2560]{1,0:T(8,128)(2,1)}), bf16[1024,2560]{1,0:T(8,128)(2,1)}) %all-gather.74.cloned.1.call-update) | async-done | bytes 5242896 | tf_op jit(solution)/shard_map/all_gather | solution.py:248
  1052.8 4.5 convolution_bitcast_fusion
  1057.3 39.1 %all-gather.70.cloned.1.call-done = bf16[1024,2560]{1,0:T(8,128)(2,1)} async-done(((bf16[128,2560]{1,0:T(8,128)(2,1)}), bf16[1024,2560]{1,0:T(8,128)(2,1)}) %all-gather.70.cloned.1.call-update) | async-done | bytes 5242896 | tf_op jit(solution)/shard_map/all_gather | solution.py:247
  1096.4 4.5 convolution_bitcast_fusion.2
  1101.0 24.9 %all-gather.64.cloned.1.call-done = bf16[1024,960]{0,1:T(8,128)(2,1)} async-done(((bf16[128,960]{0,1:T(8,128)(2,1)}), bf16[1024,960]{0,1:T(8,128)(2,1)}) %all-gather.64.cloned.1.call-update) | async-done | bytes 1966096 | tf_op jit(solution)/shard_map/all_gather | solution.py:246
  1125.8 43.0 %all-gather.72.cloned.1.call-done = bf16[1024,2560]{1,0:T(8,128)(2,1)} async-done(((bf16[128,2560]{1,0:T(8,128)(2,1)}), bf16[1024,2560]{1,0:T(8,128)(2,1)}) %all-gather.72.cloned.1.call-update) | async-done | bytes 5242896 | tf_op jit(solution)/shard_map/all_gather | solution.py:248
  1168.8 4.6 convolution_bitcast_fusion.1
  1173.5 38.4 %all-gather.66.cloned.1.call-done = bf16[1024,2560]{1,0:T(8,128)(2,1)} async-done(((bf16[128,2560]{1,0:T(8,128)(2,1)}), bf16[1024,2560]{1,0:T(8,128)(2,1)}) %all-gather.66.cloned.1.call-update) | async-done | bytes 5242896 | tf_op jit(solution)/shard_map/all_gather | solution.py:247
  1211.9 4.6 convolution_bitcast_fusion.3
  1225.3 24.6 %all-reduce.8 = (f32[960]{0:T(1024)S(1)}, f32[960]{0:T(1024)S(1)}, f32[960]{0:T(1024)S(1)}, f32[960]{0:T(1024)S(1)}) all-reduce(f32[960]{0:T(1024)S(1)} %copy-done.74, f32[960]{0:T(1024)S(1)} %get-tuple-element.17, f32[960]{0:T(1024)S(1)} %copy-done.73, f32[960]{0:T(1024)S(1)} %copy-done.75), channel_id=26, replica_groups=mesh['group'=8,'replica'=4] {'group'}, use_global_device_ids=true, to_apply=%region_22.23.clone | all-reduce | flops 3840 | bytes 30720
  1250.2 11.6 all-reduce.9
  1264.0 311.0 %all-reduce.14.cloned.1.call-done = (f32[1,120,960]{2,1,0:T(8,128)}, f32[1,120,960]{2,1,0:T(8,128)}, f32[1,120,320]{1,2,0:T(8,128)}, f32[1,120,320]{1,2,0:T(8,12...) async-done(((f32[1,120,960]{2,1,0:T(8,128)}, ...) | async-done | bytes 9830416 | tf_op jit(solution)/shard_map/psum | solution.py:140
  (381 shorter events, 151.3 us)
Async XLA Ops:
  7.2 129.2 %all-gather.82.cloned.1.call-start = ((), (), s32[]{:S(2)}) async-start(), calls=%async_computation.25 | async-start | bytes 2211840 | tf_op jit(solution)/shard_map/all_gather | solution.py:305
  9.2 143.5 %all-gather.84.cloned.1.call-start = ((), (), s32[]{:S(2)}) async-start(), calls=%async_computation.26 | async-start | bytes 2211840 | tf_op jit(solution)/shard_map/all_gather | solution.py:308
  11.3 144.2 %all-gather.86.cloned.1.call-start = ((), (), s32[]{:S(2)}) async-start(), calls=%async_computation.27 | async-start | bytes 5529600 | tf_op jit(solution)/shard_map/all_gather | solution.py:310
  12.5 149.3 %all-gather.88.cloned.1.call-start = ((), (), s32[]{:S(2)}) async-start(), calls=%async_computation.28 | async-start | bytes 5529600 | tf_op jit(solution)/shard_map/all_gather | solution.py:311
  13.7 191.5 %all-gather.90.cloned.1.call-start = ((), (), s32[]{:S(2)}) async-start(), calls=%async_computation.29 | async-start | bytes 5898240 | tf_op jit(solution)/shard_map/all_gather | solution.py:312
  15.4 21.4 %copy-start.2 = (bf16[1,128,960]{1,2,0:T(8,128)(2,1)S(1)}, bf16[1,128,960]{1,2,0:T(8,128)(2,1)}, u32[]{:S(2)}) copy-start(bf16[1,128,960]{1,2,0:T(8,128)(2,1)} %param.12) | copy-start | bytes 737284
  15.4 21.5 %copy-start.59 = (bf16[2,120,320]{1,2,0:T(8,128)(2,1)S(1)}, bf16[2,120,320]{1,2,0:T(8,128)(2,1)}, u32[]{:S(2)}) copy-start(bf16[2,120,320]{1,2,0:T(8,128)(2,1)} %param.16) | copy-start | bytes 460804
  15.4 223.4 %all-gather.92.cloned.1.call-start = ((), (), s32[]{:S(2)}) async-start(), calls=%async_computation.30 | async-start | bytes 2211840 | tf_op jit(solution)/shard_map/all_gather | solution.py:305
  16.0 252.7 %all-gather.94.cloned.1.call-start = ((), (), s32[]{:S(2)}) async-start(), calls=%async_computation.31 | async-start | bytes 2211840 | tf_op jit(solution)/shard_map/all_gather | solution.py:308
  16.7 294.2 %all-gather.98.cloned.1.call-start = ((), (), s32[]{:S(2)}) async-start(), calls=%async_computation.33 | async-start | bytes 5529600 | tf_op jit(solution)/shard_map/all_gather | solution.py:311
  17.5 337.1 %all-gather.100.cloned.1.call-start = ((), (), s32[]{:S(2)}) async-start(), calls=%async_computation.34 | async-start | bytes 5898240 | tf_op jit(solution)/shard_map/all_gather | solution.py:312
  18.2 377.9 %all-gather.96.cloned.1.call-start = ((), (), s32[]{:S(2)}) async-start(), calls=%async_computation.32 | async-start | bytes 5529600 | tf_op jit(solution)/shard_map/all_gather | solution.py:310
  18.8 452.7 %reduce-scatter.5.cloned.1.call-start = ((), (), s32[]{:S(2)}) async-start(), calls=%async_computation.4 | async-start | bytes 1474560 | tf_op jit(solution)/shard_map/reduce_scatter | solution.py:220
  36.7 103.5 %copy-start.61 = (f32[960]{0:T(1024)}, f32[960]{0:T(1024)S(1)}, u32[]{:S(2)}) copy-start(f32[960]{0:T(1024)S(1)} %convert_element_type.211) | copy-start | bytes 11524
  36.9 103.3 %copy-start.76 = (f32[128]{0:T(128)}, f32[128]{0:T(128)S(1)}, u32[]{:S(2)}) copy-start(f32[128]{0:T(128)S(1)} %add_rsqrt_fusion.3) | copy-start | bytes 1540
  49.8 13.9 copy-start.60
  52.2 25.5 %copy-start.7 = (bf16[1,960,320]{1,2,0:T(8,128)(2,1)}, bf16[1,960,320]{1,2,0:T(8,128)(2,1)S(1)}, u32[]{:S(2)}) copy-start(bf16[1,960,320]{1,2,0:T(8,128)(2,1)S(1)} %copy.49) | copy-start | bytes 1843204
  52.4 27.6 %copy-start.18 = (bf16[128,960]{0,1:T(8,128)(2,1)}, bf16[128,960]{0,1:T(8,128)(2,1)S(1)}, u32[]{:S(2)}) copy-start(bf16[128,960]{0,1:T(8,128)(2,1)S(1)} %fusion.169) | copy-start | bytes 737284
  94.8 24.7 %copy-start.53 = (bf16[1,120,320]{1,2,0:T(8,128)(2,1)S(1)}, bf16[1,120,320]{1,2,0:T(8,128)(2,1)}, u32[]{:S(2)}) copy-start(bf16[1,120,320]{1,2,0:T(8,128)(2,1)} %get-tuple-element.82) | copy-start | bytes 230404
  136.3 6.4 copy-start.63
  155.4 6.3 copy-start.9
  166.6 42.9 %copy-start.5 = (bf16[128,2560]{1,0:T(8,128)(2,1)}, bf16[128,2560]{1,0:T(8,128)(2,1)S(1)}, u32[]{:S(2)}) copy-start(bf16[128,2560]{1,0:T(8,128)(2,1)S(1)} %get-tuple-element.96) | copy-start | bytes 1966084
  209.4 14.2 copy-start.6
  209.7 29.2 %copy-start.4 = (bf16[128,960]{0,1:T(8,128)(2,1)}, bf16[128,960]{0,1:T(8,128)(2,1)S(1)}, u32[]{:S(2)}) copy-start(bf16[128,960]{0,1:T(8,128)(2,1)S(1)} %multiply_convert_fusion.7) | copy-start | bytes 737284
  224.0 17.4 %copy-start.64 = (pred[128,1024]{0,1:T(8,128)(4,1)S(1)}, pred[128,1024]{0,1:T(8,128)(4,1)}, u32[]{:S(2)}) copy-start(pred[128,1024]{0,1:T(8,128)(4,1)} %copy-done.63) | copy-start | bytes 393220
  241.4 6.9 copy-start.49
  241.4 6.9 copy-start.51
  252.6 18.6 %copy-start.33 = (bf16[5,64,3,128]{3,1,2,0:T(8,128)(2,1)}, bf16[5,64,3,128]{3,1,2,0:T(8,128)(2,1)S(1)}, u32[]{:S(2)}) copy-start(bf16[5,64,3,128]{3,1,2,0:T(8,128)(2,1)S(1)} %fusion.117) | copy-start | bytes 737284
  252.6 18.6 %copy-start.65 = (f32[960]{0:T(1024)S(1)}, f32[960]{0:T(1024)}, u32[]{:S(2)}) copy-start(f32[960]{0:T(1024)} %convert_element_type.214) | copy-start | bytes 11524
  271.4 124.7 %copy-start.19 = (bf16[128,960]{0,1:T(8,128)(2,1)}, bf16[128,960]{0,1:T(8,128)(2,1)S(1)}, u32[]{:S(2)}) copy-start(bf16[128,960]{0,1:T(8,128)(2,1)S(1)} %multiply_convert_fusion.6) | copy-start | bytes 737284
  271.7 82.9 %copy-start.12 = (bf16[1,128,960]{1,2,0:T(8,128)(2,1)S(1)}, bf16[1,128,960]{1,2,0:T(8,128)(2,1)}, u32[]{:S(2)}) copy-start(bf16[1,128,960]{1,2,0:T(8,128)(2,1)} %param.23) | copy-start | bytes 737284
  412.6 10.1 copy-start.17
  414.9 7.8 copy-start.54
  422.7 8.8 copy-start.50
  422.7 8.8 copy-start.52
  434.0 78.5 %reduce-scatter.7.cloned.1.call-start = ((), (), s32[]{:S(2)}) async-start(), calls=%async_computation.5 | async-start | bytes 1474560 | tf_op jit(solution)/shard_map/reduce_scatter | solution.py:221
  439.8 161.0 %all-gather.52.cloned.1.call-start = ((), (), s32[]{:S(2)}) async-start(), calls=%async_computation.10 | async-start | bytes 2211840 | tf_op jit(solution)/shard_map/all_gather | solution.py:240
  440.5 164.4 %all-gather.54.cloned.1.call-start = ((), (), s32[]{:S(2)}) async-start(), calls=%async_computation.11 | async-start | bytes 2211840 | tf_op jit(solution)/shard_map/all_gather | solution.py:241
  444.6 163.5 %all-gather.62.cloned.1.call-start = ((), (), s32[]{:S(2)}) async-start(), calls=%async_computation.15 | async-start | bytes 2211840 | tf_op jit(solution)/shard_map/all_gather | solution.py:245
  445.2 188.1 %all-gather.60.cloned.1.call-start = ((), (), s32[]{:S(2)}) async-start(), calls=%async_computation.14 | async-start | bytes 2211840 | tf_op jit(solution)/shard_map/all_gather | solution.py:244
  445.8 228.5 %reduce-scatter.11.cloned.1.call-start = ((), (), s32[]{:S(2)}) async-start(), calls=%async_computation.7 | async-start | bytes 1474560 | tf_op jit(solution)/shard_map/reduce_scatter | solution.py:221
  472.5 41.0 %copy-start.34 = (bf16[128,5,64]{0,2,1:T(8,128)(2,1)}, bf16[128,5,64]{0,2,1:T(8,128)(2,1)S(1)}, u32[]{:S(2)}) copy-start(bf16[128,5,64]{0,2,1:T(8,128)(2,1)S(1)} %pad_maximum_fusion.13) | copy-start | bytes 245764
  519.0 6.5 copy-start.32
  536.4 8.2 copy-start.21
  544.6 170.7 %reduce-scatter.9.cloned.1.call-start = ((), (), s32[]{:S(2)}) async-start(), calls=%async_computation.6 | async-start | bytes 1474560 | tf_op jit(solution)/shard_map/reduce_scatter | solution.py:220
  552.4 8.8 copy-start.46
  552.4 8.8 copy-start.48
  563.6 181.3 %all-gather.48.cloned.1.call-start = ((), (), s32[]{:S(2)}) async-start(), calls=%async_computation.8 | async-start | bytes 2211840 | tf_op jit(solution)/shard_map/all_gather | solution.py:240
  564.3 210.5 %all-gather.50.cloned.1.call-start = ((), (), s32[]{:S(2)}) async-start(), calls=%async_computation.9 | async-start | bytes 2211840 | tf_op jit(solution)/shard_map/all_gather | solution.py:241
  568.3 236.0 %all-gather.56.cloned.1.call-start = ((), (), s32[]{:S(2)}) async-start(), calls=%async_computation.12 | async-start | bytes 2211840 | tf_op jit(solution)/shard_map/all_gather | solution.py:244
  569.0 265.4 %all-gather.58.cloned.1.call-start = ((), (), s32[]{:S(2)}) async-start(), calls=%async_computation.13 | async-start | bytes 2211840 | tf_op jit(solution)/shard_map/all_gather | solution.py:245
  569.8 294.2 %all-gather.78.cloned.1.call-start = ((), (), s32[]{:S(2)}) async-start(), calls=%async_computation.23 | async-start | bytes 2211840 | tf_op jit(solution)/shard_map/all_gather | solution.py:250
  570.5 336.3 %all-gather.76.cloned.1.call-start = ((), (), s32[]{:S(2)}) async-start(), calls=%async_computation.22 | async-start | bytes 5898240 | tf_op jit(solution)/shard_map/all_gather | solution.py:249
  571.1 365.3 %all-gather.102.cloned.1.call-start = ((), (), s32[]{:S(2)}) async-start(), calls=%async_computation.35 | async-start | bytes 2211840 | tf_op jit(solution)/shard_map/all_gather | solution.py:250
  571.9 408.0 %all-gather.80.cloned.1.call-start = ((), (), s32[]{:S(2)}) async-start(), calls=%async_computation.24 | async-start | bytes 5898240 | tf_op jit(solution)/shard_map/all_gather | solution.py:249
  572.4 15.7 copy-start.37
  572.4 436.8 %all-gather.68.cloned.1.call-start = ((), (), s32[]{:S(2)}) async-start(), calls=%async_computation.18 | async-start | bytes 2211840 | tf_op jit(solution)/shard_map/all_gather | solution.py:246
  573.0 479.8 %all-gather.74.cloned.1.call-start = ((), (), s32[]{:S(2)}) async-start(), calls=%async_computation.21 | async-start | bytes 5898240 | tf_op jit(solution)/shard_map/all_gather | solution.py:248
  573.8 522.7 %all-gather.70.cloned.1.call-start = ((), (), s32[]{:S(2)}) async-start(), calls=%async_computation.19 | async-start | bytes 5898240 | tf_op jit(solution)/shard_map/all_gather | solution.py:247
  574.5 551.3 %all-gather.64.cloned.1.call-start = ((), (), s32[]{:S(2)}) async-start(), calls=%async_computation.16 | async-start | bytes 2211840 | tf_op jit(solution)/shard_map/all_gather | solution.py:246
  575.1 593.8 %all-gather.72.cloned.1.call-start = ((), (), s32[]{:S(2)}) async-start(), calls=%async_computation.20 | async-start | bytes 5898240 | tf_op jit(solution)/shard_map/all_gather | solution.py:248
  575.8 636.1 %all-gather.66.cloned.1.call-start = ((), (), s32[]{:S(2)}) async-start(), calls=%async_computation.17 | async-start | bytes 5898240 | tf_op jit(solution)/shard_map/all_gather | solution.py:247
  576.6 998.4 %all-reduce.14.cloned.1.call-start = ((), (), s32[]{:S(2)}) async-start(), calls=%async_computation.36 | async-start | bytes 20316160 | tf_op jit(solution)/shard_map/psum | solution.py:140
  1224.5 38.5 %copy-start.23 = (f32[128,960]{0,1:T(8,128)S(1)}, f32[128,960]{0,1:T(8,128)}, u32[]{:S(2)}) copy-start(f32[128,960]{0,1:T(8,128)} %get-tuple-element.46) | copy-start | bytes 1474564
  (65 other events, 193.7 us)
Sparse Core Ops, SparseCore 0:
  10.5 30.1 all-gather.81
  42.5 27.3 all-gather.83
  72.4 47.8 all-gather.85
  122.0 39.7 all-gather.87
  164.1 41.1 all-gather.89
  207.5 31.2 all-gather.91
  241.3 27.4 all-gather.93
  271.2 39.7 all-gather.97
  313.4 41.1 all-gather.99
  356.3 39.7 all-gather.95
  434.1 37.3 reduce-scatter.4
  475.2 37.3 reduce-scatter.6
  514.4 27.5 all-gather.51
  544.4 27.6 all-gather.53
  573.7 30.1 all-gather.61
  605.7 27.5 all-gather.59
  636.9 37.3 reduce-scatter.10
  678.0 37.3 reduce-scatter.8
  717.2 27.5 all-gather.47
  747.1 27.6 all-gather.49
  776.7 27.6 all-gather.55
  806.8 27.6 all-gather.57
  836.3 27.6 all-gather.77
  865.7 41.1 all-gather.75
  908.7 27.6 all-gather.101
  938.7 41.1 all-gather.79
  981.6 27.6 all-gather.67
  1011.7 41.1 all-gather.73
  1055.3 41.1 all-gather.69
  1098.2 27.6 all-gather.63
  1127.7 41.1 all-gather.71
  1170.7 41.1 all-gather.65
  1217.5 357.5 all-reduce.13
where the time goes:
time: 1600 us; the launch traced here: 1590 us
  waiting for transfers between devices  1100 us (69%)
  blocking collectives  205 us (13%)
  matrix products  191 us (12%)
  other arithmetic  38.1 us (2%)
  local copies, waits for them, and re-layouts  36.4 us (2%)
  between operations  17.4 us (1%)
    psum x1, waiting for transfers between devices, replica_total(): lax.psum((share_gain_attn, share_query, share_key, share_value, share_out...  311 us
    all_gather x2, waiting for transfers between devices, layer_backward(): piece_up = lax.all_gather(grad_up_low, 'group', axis=0, tiled=True)  86.6 us
    all_gather x2, waiting for transfers between devices, layer_backward(): piece_hidden = lax.all_gather(hidden, 'group', axis=0, tiled=True)  86.4 us
    all_gather x2, waiting for transfers between devices, on_device(): lax.all_gather(w_down[layer_index], 'group', axis=0, tiled=True)  78 us
    all_gather x2, waiting for transfers between devices, layer_backward(): piece_gate = lax.all_gather(grad_gate_low, 'group', axis=0, tiled=True)  77.5 us
    reduce_scatter x2, waiting for transfers between devices, layer_backward(): lax.psum_scatter(grad_value_all, 'group', scatter_dimension=0, tiled=True)  75.5 us
    reduce_scatter x2, waiting for transfers between devices, layer_backward(): lax.psum_scatter(grad_key_all, 'group', scatter_dimension=0, tiled=True)  65.6 us
    all_gather x2, waiting for transfers between devices, layer_backward(): piece_branch = lax.all_gather(branch_low, 'group', axis=0, tiled=True)  51.5 us
  transfers between devices with their start and end apart: 33, of which 27 were waited for; matrix products, arithmetic and copies ran while one was open for 13% of the time, Pallas kernels for 0%

commit v1 on v0

--- a/solution.py
+++ b/solution.py
@@ -243,7 +243,14 @@
     piece_value = lax.all_gather(value_back, "group", axis=0, tiled=True)
     piece_mixed = lax.all_gather(mixed_heads, "group", axis=0, tiled=True)
     piece_after = lax.all_gather(after_low, "group", axis=0, tiled=True)
-    piece_ffn = lax.all_gather(normed_ffn, "group", axis=0, tiled=True)
+    ring = [normed_ffn]
+    for hop in range(7):
+        ring.append(lax.ppermute(ring[-1], "group", [(dev, (dev + 1) % 8) for dev in range(8)]))
+    piece_ffn = jnp.roll(
+        jnp.concatenate(ring[::-1], axis=0),
+        (lax.axis_index("group") + 1) * ring[0].shape[0],
+        axis=0,
+    )
     piece_gate = lax.all_gather(grad_gate_low, "group", axis=0, tiled=True)
     piece_up = lax.all_gather(grad_up_low, "group", axis=0, tiled=True)
     piece_hidden = lax.all_gather(hidden, "group", axis=0, tiled=True)

time: 1600 us -> 1540 us (0.963)
  waiting for transfers between devices: 1100 us -> 1020 us
    ppermute x0 -> x14, waiting for transfers between devices: none -> 68.9 us  [layer_backward(): lax.ppermute(ring[-1], 'group', [(dev, (dev + 1) % 8) for dev in range(8)])]
    reduce_scatter x2, waiting for transfers between devices: 75.5 us -> 12 us  [layer_backward(): lax.psum_scatter(grad_value_all, 'group', scatter_dimension=0, tiled=True)]
    all_gather x2 -> x0, waiting for transfers between devices: 49.9 us -> none  [layer_backward(): piece_ffn = lax.all_gather(normed_ffn, 'group', axis=0, tiled=True)]
    all_gather x2, waiting for transfers between devices: 51.4 us -> 26.3 us  [layer_backward(): piece_mixed = lax.all_gather(mixed_heads, 'group', axis=0, tiled=True)]
  transfers between devices with their start and end apart: 33 -> 45, of which waited for: 27 -> 36; matrix products, arithmetic and copies ran while one was open for 13% -> 15% of each run, Pallas kernels for 0% -> 0%
where the time goes in v1:
time: 1540 us; the launch traced here: 1530 us
  waiting for transfers between devices  1020 us (66%)
  blocking collectives  208 us (14%)
  matrix products  190 us (12%)
  local copies, waits for them, and re-layouts  48.1 us (3%)
  other arithmetic  38.8 us (3%)
  between operations  17.7 us (1%)
    psum x1, waiting for transfers between devices, replica_total(): lax.psum((share_gain_attn, share_query, share_key, share_value, share_out...  311 us
    all_gather x2, waiting for transfers between devices, layer_backward(): piece_hidden = lax.all_gather(hidden, 'group', axis=0, tiled=True)  86.4 us
    all_gather x2, waiting for transfers between devices, layer_backward(): piece_gate = lax.all_gather(grad_gate_low, 'group', axis=0, tiled=True)  78.1 us
    all_gather x2, waiting for transfers between devices, layer_backward(): piece_up = lax.all_gather(grad_up_low, 'group', axis=0, tiled=True)  76.7 us
    all_gather x2, waiting for transfers between devices, on_device(): lax.all_gather(w_down[layer_index], 'group', axis=0, tiled=True)  73 us
    reduce_scatter x2, waiting for transfers between devices, layer_backward(): lax.psum_scatter(grad_key_all, 'group', scatter_dimension=0, tiled=True)  71.2 us
    ppermute x14, waiting for transfers between devices, layer_backward(): lax.ppermute(ring[-1], 'group', [(dev, (dev + 1) % 8) for dev in range(8)])  68.9 us
    all_gather x2, waiting for transfers between devices, layer_backward(): piece_branch = lax.all_gather(branch_low, 'group', axis=0, tiled=True)  51.5 us
  transfers between devices with their start and end apart: 45, of which 36 were waited for; matrix products, arithmetic and copies ran while one was open for 15% of the time, Pallas kernels for 0%

profile of v1, /device:TPU:0, one launch (start us, length us, event | category | flops | bytes accessed | tf_op | source)
XLA Modules:
  0.0 1527.6 jit_solution(2595228946666722594)
XLA Ops:
  21.0 15.6 %all-reduce.11 = (bf16[960]{0:T(1024)(128)(2,1)S(1)}, bf16[960]{0:T(1024)(128)(2,1)S(1)}, bf16[960]{0:T(1024)(128)(2,1)S(1)}, bf16[960]{0:T(1024)(128)(2,1)S(1)}) all-reduce(bf16[960]{0:T(1024)(128)(2,1)S(1)} %dynamic-update-slice, bf16[960]{0:T(1024)(128)(2,1)S(1)} %dynamic-update-slice.1, ...), channel_id=2, replica_groups=mesh['group'=8,'replica'=4] {'group'}, use_global_device_ids=true, to_apply=%add | all-reduce | flops 3840 | bytes 15360
  37.1 12.7 all-gather.1
  53.9 10.7 all_gather.150
  64.9 15.5 %all-gather.2 = bf16[1,960,320]{2,0,1:T(2,128)(2,1)} all-gather(bf16[1,120,320]{2,0,1:T(2,128)(2,1)S(1)} %copy.80), channel_id=4, replica_groups=mesh['group'=8,'replica'=4] {'group'}, dimensions={1}, use_global_device_ids=true | all-gather | bytes 691200 | tf_op jit(solution)/shard_map/all_gather | solution.py:313
  84.6 11.0 all_gather.152
  96.5 20.6 %all-gather.10 = bf16[1,960,320]{2,0,1:T(2,128)(2,1)} all-gather(bf16[1,120,320]{2,0,1:T(2,128)(2,1)S(1)} %copy.81), channel_id=12, replica_groups=mesh['group'=8,'replica'=4] {'group'}, dimensions={1}, use_global_device_ids=true | all-gather | bytes 691200 | tf_op jit(solution)/shard_map/all_gather | solution.py:314
  117.1 4.6 copy.53
  121.9 18.1 %all-gather.11 = bf16[1,960,320]{2,0,1:T(2,128)(2,1)} all-gather(bf16[1,120,320]{2,0,1:T(2,128)(2,1)S(1)} %copy.82), channel_id=13, replica_groups=mesh['group'=8,'replica'=4] {'group'}, dimensions={1}, use_global_device_ids=true | all-gather | bytes 691200 | tf_op jit(solution)/shard_map/all_gather | solution.py:313
  140.0 4.6 copy.55
  151.7 5.8 fusion.234
  168.8 4.8 multiply_convert_fusion.5
  173.6 33.8 %all-gather.84.cloned.1.call-done = bf16[1,2560,960]{2,1,0:T(8,128)(2,1)} async-done(((bf16[1,320,960]{2,1,0:T(8,128)(2,1)}), bf16[1,2560,960]{2,1,0:T(8,128)(2,1)}) %all-gather.84.cloned.1.call-update) | async-done | bytes 4915216 | tf_op jit(solution)/shard_map/all_gather | solution.py:319
  213.9 11.9 all_gather.161
  225.8 13.8 all_gather.163
  242.9 6.7 fusion.239
  254.0 16.2 %all-gather.88.cloned.1.call-done = bf16[1,960,960]{2,1,0:T(8,128)(2,1)} async-done(((bf16[1,120,960]{2,1,0:T(8,128)(2,1)}), bf16[1,960,960]{2,1,0:T(8,128)(2,1)}) %all-gather.88.cloned.1.call-update) | async-done | bytes 1843216 | tf_op jit(solution)/shard_map/all_gather | solution.py:315
  272.9 39.5 %all-gather.92.cloned.1.call-done = bf16[1,960,2560]{2,1,0:T(8,128)(2,1)} async-done(((bf16[1,120,2560]{2,1,0:T(8,128)(2,1)}), bf16[1,960,2560]{2,1,0:T(8,128)(2,1)}) %all-gather.92.cloned.1.call-update) | async-done | bytes 4915216 | tf_op jit(solution)/shard_map/all_gather | solution.py:318
  316.8 39.2 %all-gather.94.cloned.1.call-done = bf16[1,2560,960]{2,1,0:T(8,128)(2,1)} async-done(((bf16[1,320,960]{2,1,0:T(8,128)(2,1)}), bf16[1,2560,960]{2,1,0:T(8,128)(2,1)}) %all-gather.94.cloned.1.call-update) | async-done | bytes 4915216 | tf_op jit(solution)/shard_map/all_gather | solution.py:319
  356.1 5.4 fusion.10
  361.5 36.1 %all-gather.90.cloned.1.call-done = bf16[1,960,2560]{2,1,0:T(8,128)(2,1)} async-done(((bf16[1,120,2560]{2,1,0:T(8,128)(2,1)}), bf16[1,960,2560]{2,1,0:T(8,128)(2,1)}) %all-gather.90.cloned.1.call-update) | async-done | bytes 4915216 | tf_op jit(solution)/shard_map/all_gather | solution.py:317
  397.6 5.7 multiply_convert_fusion.3
  403.3 4.8 fusion.18
  408.1 4.8 multiply_reduce_fusion
  416.8 5.9 fusion.71
  422.8 7.7 fusion.5
  430.5 7.3 fusion.7
  448.2 12.0 reduce-scatter.7.cloned.1.call-done
  464.1 36.6 %reduce-scatter.5.cloned.1.call-done = f32[128,5,64]{0,2,1:T(8,128)} async-done(((f32[1024,5,64]{0,2,1:T(8,128)}), f32[128,5,64]{0,2,1:T(8,128)}) %reduce-scatter.5.cloned.1.call-update) | async-done | bytes 163856 | tf_op jit(solution)/shard_map/reduce_scatter | solution.py:220
  507.2 6.4 multiply_convert_fusion.1
  513.6 4.8 fusion.26
  518.5 5.1 multiply_reduce_fusion.1
  527.6 5.9 fusion.68
  533.6 7.8 fusion.2
  541.3 6.9 fusion.4
  564.5 6.5 collective-permute-done
  571.0 7.1 collective-permute-done.1
  578.1 7.1 collective-permute-done.2
  585.2 7.3 collective-permute-done.7
  605.7 5.3 collective-permute-done.5
  626.4 5.3 collective-permute-done.12
  632.1 6.1 collective-permute-done.13
  641.0 9.7 all_gather.175
  650.7 12.0 all_gather.177
  674.3 34.6 %reduce-scatter.9.cloned.1.call-done = f32[128,5,64]{0,2,1:T(8,128)} async-done(((f32[1024,5,64]{0,2,1:T(8,128)}), f32[128,5,64]{0,2,1:T(8,128)}) %reduce-scatter.9.cloned.1.call-update) | async-done | bytes 163856 | tf_op jit(solution)/shard_map/reduce_scatter | solution.py:220
  709.9 11.2 all_gather.174
  721.1 9.4 all_gather.176
  730.5 8.0 all-gather.46.cloned.1.call-done
  742.7 25.2 %all-gather.48.cloned.1.call-done = bf16[1024,960]{0,1:T(8,128)(2,1)} async-done(((bf16[128,960]{0,1:T(8,128)(2,1)}), bf16[1024,960]{0,1:T(8,128)(2,1)}) %all-gather.48.cloned.1.call-update) | async-done | bytes 1966096 | tf_op jit(solution)/shard_map/all_gather | solution.py:241
  771.1 26.3 %all-gather.54.cloned.1.call-done = bf16[1024,960]{0,1:T(8,128)(2,1)} async-done(((bf16[128,960]{0,1:T(8,128)(2,1)}), bf16[1024,960]{0,1:T(8,128)(2,1)}) %all-gather.54.cloned.1.call-update) | async-done | bytes 1966096 | tf_op jit(solution)/shard_map/all_gather | solution.py:244
  797.4 29.5 %all-gather.56.cloned.1.call-done = bf16[1024,960]{0,1:T(8,128)(2,1)} async-done(((bf16[128,960]{0,1:T(8,128)(2,1)}), bf16[1024,960]{0,1:T(8,128)(2,1)}) %all-gather.56.cloned.1.call-update) | async-done | bytes 1966096 | tf_op jit(solution)/shard_map/all_gather | solution.py:245
  830.2 26.3 %all-gather.96.cloned.1.call-done = bf16[1,1024,960]{1,2,0:T(8,128)(2,1)} async-done(((bf16[1,128,960]{1,2,0:T(8,128)(2,1)}), bf16[1,1024,960]{1,2,0:T(8,128)(2,1)}) %all-gather.96.cloned.1.call-update) | async-done | bytes 1966096 | tf_op jit(solution)/shard_map/all_gather | solution.py:257
  856.4 43.5 %all-gather.74.cloned.1.call-done = bf16[1024,2560]{1,0:T(8,128)(2,1)} async-done(((bf16[128,2560]{1,0:T(8,128)(2,1)}), bf16[1024,2560]{1,0:T(8,128)(2,1)}) %all-gather.74.cloned.1.call-update) | async-done | bytes 5242896 | tf_op jit(solution)/shard_map/all_gather | solution.py:256
  904.2 25.2 %all-gather.72.cloned.1.call-done = bf16[1024,960]{0,1:T(8,128)(2,1)} async-done(((bf16[128,960]{0,1:T(8,128)(2,1)}), bf16[1024,960]{0,1:T(8,128)(2,1)}) %all-gather.72.cloned.1.call-update) | async-done | bytes 1966096 | tf_op jit(solution)/shard_map/all_gather | solution.py:257
  929.4 42.9 %all-gather.70.cloned.1.call-done = bf16[1024,2560]{1,0:T(8,128)(2,1)} async-done(((bf16[128,2560]{1,0:T(8,128)(2,1)}), bf16[1024,2560]{1,0:T(8,128)(2,1)}) %all-gather.70.cloned.1.call-update) | async-done | bytes 5242896 | tf_op jit(solution)/shard_map/all_gather | solution.py:256
  976.6 39.1 %all-gather.64.cloned.1.call-done = bf16[1024,2560]{1,0:T(8,128)(2,1)} async-done(((bf16[128,2560]{1,0:T(8,128)(2,1)}), bf16[1024,2560]{1,0:T(8,128)(2,1)}) %all-gather.64.cloned.1.call-update) | async-done | bytes 5242896 | tf_op jit(solution)/shard_map/all_gather | solution.py:254
  1015.8 4.6 convolution_bitcast_fusion.2
  1020.4 38.4 %all-gather.68.cloned.1.call-done = bf16[1024,2560]{1,0:T(8,128)(2,1)} async-done(((bf16[128,2560]{1,0:T(8,128)(2,1)}), bf16[1024,2560]{1,0:T(8,128)(2,1)}) %all-gather.68.cloned.1.call-update) | async-done | bytes 5242896 | tf_op jit(solution)/shard_map/all_gather | solution.py:255
  1058.8 4.6 convolution_bitcast_fusion
  1063.4 39.0 %all-gather.62.cloned.1.call-done = bf16[1024,2560]{1,0:T(8,128)(2,1)} async-done(((bf16[128,2560]{1,0:T(8,128)(2,1)}), bf16[1024,2560]{1,0:T(8,128)(2,1)}) %all-gather.62.cloned.1.call-update) | async-done | bytes 5242896 | tf_op jit(solution)/shard_map/all_gather | solution.py:254
  1107.0 38.3 %all-gather.66.cloned.1.call-done = bf16[1024,2560]{1,0:T(8,128)(2,1)} async-done(((bf16[128,2560]{1,0:T(8,128)(2,1)}), bf16[1024,2560]{1,0:T(8,128)(2,1)}) %all-gather.66.cloned.1.call-update) | async-done | bytes 5242896 | tf_op jit(solution)/shard_map/all_gather | solution.py:255
  1145.3 4.6 convolution_bitcast_fusion.1
  1158.7 24.6 %all-reduce.8 = (f32[960]{0:T(1024)S(1)}, f32[960]{0:T(1024)S(1)}, f32[960]{0:T(1024)S(1)}, f32[960]{0:T(1024)S(1)}) all-reduce(f32[960]{0:T(1024)S(1)} %copy-done.84, f32[960]{0:T(1024)S(1)} %get-tuple-element.18, f32[960]{0:T(1024)S(1)} %copy-done.83, f32[960]{0:T(1024)S(1)} %copy-done.85), channel_id=26, replica_groups=mesh['group'=8,'replica'=4] {'group'}, use_global_device_ids=true, to_apply=%region_22.23.clone | all-reduce | flops 3840 | bytes 30720
  1183.6 11.7 all-reduce.9
  1197.4 311.2 %all-reduce.14.cloned.1.call-done = (f32[1,120,960]{2,1,0:T(8,128)}, f32[1,120,960]{2,1,0:T(8,128)}, f32[1,120,320]{1,2,0:T(8,128)}, f32[1,120,320]{1,2,0:T(8,12...) async-done(((f32[1,120,960]{2,1,0:T(8,128)}, ...) | async-done | bytes 9830416 | tf_op jit(solution)/shard_map/psum | solution.py:140
  (443 shorter events, 197.0 us)
Async XLA Ops:
  7.2 138.2 %all-gather.76.cloned.1.call-start = ((), (), s32[]{:S(2)}) async-start(), calls=%async_computation.23 | async-start | bytes 2211840 | tf_op jit(solution)/shard_map/all_gather | solution.py:312
  9.2 152.4 %all-gather.78.cloned.1.call-start = ((), (), s32[]{:S(2)}) async-start(), calls=%async_computation.24 | async-start | bytes 2211840 | tf_op jit(solution)/shard_map/all_gather | solution.py:315
  11.3 153.2 %all-gather.80.cloned.1.call-start = ((), (), s32[]{:S(2)}) async-start(), calls=%async_computation.25 | async-start | bytes 5529600 | tf_op jit(solution)/shard_map/all_gather | solution.py:317
  12.5 156.3 %all-gather.82.cloned.1.call-start = ((), (), s32[]{:S(2)}) async-start(), calls=%async_computation.26 | async-start | bytes 5529600 | tf_op jit(solution)/shard_map/all_gather | solution.py:318
  13.7 193.6 %all-gather.84.cloned.1.call-start = ((), (), s32[]{:S(2)}) async-start(), calls=%async_computation.27 | async-start | bytes 5898240 | tf_op jit(solution)/shard_map/all_gather | solution.py:319
  15.3 21.4 %copy-start.2 = (bf16[1,128,960]{1,2,0:T(8,128)(2,1)S(1)}, bf16[1,128,960]{1,2,0:T(8,128)(2,1)}, u32[]{:S(2)}) copy-start(bf16[1,128,960]{1,2,0:T(8,128)(2,1)} %param.14) | copy-start | bytes 737284
  15.4 21.5 %copy-start.68 = (bf16[2,120,320]{1,2,0:T(8,128)(2,1)S(1)}, bf16[2,120,320]{1,2,0:T(8,128)(2,1)}, u32[]{:S(2)}) copy-start(bf16[2,120,320]{1,2,0:T(8,128)(2,1)} %param.19) | copy-start | bytes 460804
  15.4 224.9 %all-gather.86.cloned.1.call-start = ((), (), s32[]{:S(2)}) async-start(), calls=%async_computation.28 | async-start | bytes 2211840 | tf_op jit(solution)/shard_map/all_gather | solution.py:312
  16.0 254.3 %all-gather.88.cloned.1.call-start = ((), (), s32[]{:S(2)}) async-start(), calls=%async_computation.29 | async-start | bytes 2211840 | tf_op jit(solution)/shard_map/all_gather | solution.py:315
  16.7 295.7 %all-gather.92.cloned.1.call-start = ((), (), s32[]{:S(2)}) async-start(), calls=%async_computation.31 | async-start | bytes 5529600 | tf_op jit(solution)/shard_map/all_gather | solution.py:318
  17.5 338.6 %all-gather.94.cloned.1.call-start = ((), (), s32[]{:S(2)}) async-start(), calls=%async_computation.32 | async-start | bytes 5898240 | tf_op jit(solution)/shard_map/all_gather | solution.py:319
  18.2 379.4 %all-gather.90.cloned.1.call-start = ((), (), s32[]{:S(2)}) async-start(), calls=%async_computation.30 | async-start | bytes 5529600 | tf_op jit(solution)/shard_map/all_gather | solution.py:317
  18.8 441.4 %reduce-scatter.7.cloned.1.call-start = ((), (), s32[]{:S(2)}) async-start(), calls=%async_computation.5 | async-start | bytes 1474560 | tf_op jit(solution)/shard_map/reduce_scatter | solution.py:221
  36.7 112.6 %copy-start.74 = (f32[960]{0:T(1024)}, f32[960]{0:T(1024)S(1)}, u32[]{:S(2)}) copy-start(f32[960]{0:T(1024)S(1)} %convert_element_type.211) | copy-start | bytes 11524
  36.9 112.4 %copy-start.90 = (f32[128]{0:T(128)}, f32[128]{0:T(128)S(1)}, u32[]{:S(2)}) copy-start(f32[128]{0:T(128)S(1)} %add_rsqrt_fusion.3) | copy-start | bytes 1540
  53.6 26.8 %copy-start.22 = (bf16[128,960]{0,1:T(8,128)(2,1)}, bf16[128,960]{0,1:T(8,128)(2,1)S(1)}, u32[]{:S(2)}) copy-start(bf16[128,960]{0,1:T(8,128)(2,1)S(1)} %fusion.169) | copy-start | bytes 737284
  84.0 33.2 %copy-start.10 = (bf16[1,960,320]{1,2,0:T(8,128)(2,1)}, bf16[1,960,320]{1,2,0:T(8,128)(2,1)S(1)}, u32[]{:S(2)}) copy-start(bf16[1,960,320]{1,2,0:T(8,128)(2,1)S(1)} %copy.49) | copy-start | bytes 1843204
  95.6 56.1 %copy-start.15 = (bf16[1024,5,64]{0,2,1:T(8,128)(2,1)}, bf16[1024,5,64]{0,2,1:T(8,128)(2,1)S(1)}, u32[]{:S(2)}) copy-start(bf16[1024,5,64]{0,2,1:T(8,128)(2,1)S(1)} %all_gather.152) | copy-start | bytes 1966084
  95.6 68.6 %copy-start.77 = (f32[960]{0:T(1024)}, f32[960]{0:T(1024)S(1)}, u32[]{:S(2)}) copy-start(f32[960]{0:T(1024)S(1)} %convert_element_type.212) | copy-start | bytes 11524
  173.6 38.0 %copy-start.7 = (bf16[128,2560]{1,0:T(8,128)(2,1)}, bf16[128,2560]{1,0:T(8,128)(2,1)S(1)}, u32[]{:S(2)}) copy-start(bf16[128,2560]{1,0:T(8,128)(2,1)S(1)} %get-tuple-element.97) | copy-start | bytes 1966084
  211.8 28.5 %copy-start.6 = (bf16[128,960]{0,1:T(8,128)(2,1)}, bf16[128,960]{0,1:T(8,128)(2,1)S(1)}, u32[]{:S(2)}) copy-start(bf16[128,960]{0,1:T(8,128)(2,1)S(1)} %multiply_convert_fusion.7) | copy-start | bytes 737284
  254.0 18.7 %copy-start.70 = (f32[960]{0:T(1024)S(1)}, f32[960]{0:T(1024)}, u32[]{:S(2)}) copy-start(f32[960]{0:T(1024)} %convert_element_type.214) | copy-start | bytes 11524
  272.7 44.2 %copy-start.86 = (f32[128]{0:T(128)}, f32[128]{0:T(128)S(1)}, u32[]{:S(2)}) copy-start(f32[128]{0:T(128)S(1)} %add_rsqrt_fusion) | copy-start | bytes 1540
  272.9 43.9 %copy-start.38 = (bf16[128,960]{0,1:T(8,128)(2,1)}, bf16[128,960]{0,1:T(8,128)(2,1)S(1)}, u32[]{:S(2)}) copy-start(bf16[128,960]{0,1:T(8,128)(2,1)S(1)} %multiply_convert_fusion.6) | copy-start | bytes 737284
  272.9 83.2 %copy-start.14 = (bf16[1,128,960]{1,2,0:T(8,128)(2,1)S(1)}, bf16[1,128,960]{1,2,0:T(8,128)(2,1)}, u32[]{:S(2)}) copy-start(bf16[1,128,960]{1,2,0:T(8,128)(2,1)} %param.25) | copy-start | bytes 737284
  422.7 77.9 %reduce-scatter.5.cloned.1.call-start = ((), (), s32[]{:S(2)}) async-start(), calls=%async_computation.4 | async-start | bytes 1474560 | tf_op jit(solution)/shard_map/reduce_scatter | solution.py:220
  442.2 220.4 %all-gather.50.cloned.1.call-start = ((), (), s32[]{:S(2)}) async-start(), calls=%async_computation.10 | async-start | bytes 2211840 | tf_op jit(solution)/shard_map/all_gather | solution.py:240
  443.0 223.9 %all-gather.52.cloned.1.call-start = ((), (), s32[]{:S(2)}) async-start(), calls=%async_computation.11 | async-start | bytes 2211840 | tf_op jit(solution)/shard_map/all_gather | solution.py:241
  446.2 56.2 %copy-start.8 = (bf16[1,960,320]{1,2,0:T(8,128)(2,1)S(1)}, bf16[1,960,320]{1,2,0:T(8,128)(2,1)}, u32[]{:S(2)}) copy-start(bf16[1,960,320]{1,2,0:T(8,128)(2,1)} %copy.55) | copy-start | bytes 1843204
  447.0 223.2 %all-gather.60.cloned.1.call-start = ((), (), s32[]{:S(2)}) async-start(), calls=%async_computation.15 | async-start | bytes 2211840 | tf_op jit(solution)/shard_map/all_gather | solution.py:245
  447.6 222.6 %all-gather.58.cloned.1.call-start = ((), (), s32[]{:S(2)}) async-start(), calls=%async_computation.14 | async-start | bytes 2211840 | tf_op jit(solution)/shard_map/all_gather | solution.py:244
  448.2 225.2 %reduce-scatter.11.cloned.1.call-start = ((), (), s32[]{:S(2)}) async-start(), calls=%async_computation.7 | async-start | bytes 1474560 | tf_op jit(solution)/shard_map/reduce_scatter | solution.py:221
  533.5 175.5 %reduce-scatter.9.cloned.1.call-start = ((), (), s32[]{:S(2)}) async-start(), calls=%async_computation.6 | async-start | bytes 1474560 | tf_op jit(solution)/shard_map/reduce_scatter | solution.py:220
  552.6 185.8 %all-gather.46.cloned.1.call-start = ((), (), s32[]{:S(2)}) async-start(), calls=%async_computation.8 | async-start | bytes 2211840 | tf_op jit(solution)/shard_map/all_gather | solution.py:240
  553.4 214.5 %all-gather.48.cloned.1.call-start = ((), (), s32[]{:S(2)}) async-start(), calls=%async_computation.9 | async-start | bytes 2211840 | tf_op jit(solution)/shard_map/all_gather | solution.py:241
  557.4 240.0 %all-gather.54.cloned.1.call-start = ((), (), s32[]{:S(2)}) async-start(), calls=%async_computation.12 | async-start | bytes 2211840 | tf_op jit(solution)/shard_map/all_gather | solution.py:244
  558.1 268.8 %all-gather.56.cloned.1.call-start = ((), (), s32[]{:S(2)}) async-start(), calls=%async_computation.13 | async-start | bytes 2211840 | tf_op jit(solution)/shard_map/all_gather | solution.py:245
  558.9 297.6 %all-gather.96.cloned.1.call-start = ((), (), s32[]{:S(2)}) async-start(), calls=%async_computation.33 | async-start | bytes 2211840 | tf_op jit(solution)/shard_map/all_gather | solution.py:257
  559.6 340.3 %all-gather.74.cloned.1.call-start = ((), (), s32[]{:S(2)}) async-start(), calls=%async_computation.22 | async-start | bytes 5898240 | tf_op jit(solution)/shard_map/all_gather | solution.py:256
  560.2 369.3 %all-gather.72.cloned.1.call-start = ((), (), s32[]{:S(2)}) async-start(), calls=%async_computation.21 | async-start | bytes 2211840 | tf_op jit(solution)/shard_map/all_gather | solution.py:257
  560.9 411.4 %all-gather.70.cloned.1.call-start = ((), (), s32[]{:S(2)}) async-start(), calls=%async_computation.20 | async-start | bytes 5898240 | tf_op jit(solution)/shard_map/all_gather | solution.py:256
  561.5 454.3 %all-gather.64.cloned.1.call-start = ((), (), s32[]{:S(2)}) async-start(), calls=%async_computation.17 | async-start | bytes 5898240 | tf_op jit(solution)/shard_map/all_gather | solution.py:254
  562.1 496.7 %all-gather.68.cloned.1.call-start = ((), (), s32[]{:S(2)}) async-start(), calls=%async_computation.19 | async-start | bytes 5898240 | tf_op jit(solution)/shard_map/all_gather | solution.py:255
  562.8 539.6 %all-gather.62.cloned.1.call-start = ((), (), s32[]{:S(2)}) async-start(), calls=%async_computation.16 | async-start | bytes 5898240 | tf_op jit(solution)/shard_map/all_gather | solution.py:254
  563.6 68.2 %copy-start.80 = (f32[960]{0:T(1024)S(1)}, f32[960]{0:T(1024)}, u32[]{:S(2)}) copy-start(f32[960]{0:T(1024)} %copy-done.77) | copy-start | bytes 11524
  563.6 68.2 %copy-start.99 = (f32[128]{0:T(128)S(1)}, f32[128]{0:T(128)}, u32[]{:S(2)}) copy-start(f32[128]{0:T(128)} %copy-done.96) | copy-start | bytes 1540
  563.6 581.7 %all-gather.66.cloned.1.call-start = ((), (), s32[]{:S(2)}) async-start(), calls=%async_computation.18 | async-start | bytes 5898240 | tf_op jit(solution)/shard_map/all_gather | solution.py:255
  564.2 944.4 %all-reduce.14.cloned.1.call-start = ((), (), s32[]{:S(2)}) async-start(), calls=%async_computation.34 | async-start | bytes 20316160 | tf_op jit(solution)/shard_map/psum | solution.py:140
  564.4 6.6 collective-permute-start
  571.0 7.1 collective-permute-start.1
  578.1 7.1 collective-permute-start.2
  578.1 14.4 collective-permute-start.7
  585.2 20.5 %copy-start.58 = (bf16[128,960]{0,1:T(8,128)(2,1)}, bf16[128,960]{0,1:T(8,128)(2,1)S(1)}, u32[]{:S(2)}) copy-start(bf16[128,960]{0,1:T(8,128)(2,1)S(1)} %collective-permute-done.2) | copy-start | bytes 737284
  585.2 9.9 collective-permute-start.3
  592.5 6.5 collective-permute-start.8
  595.2 6.5 collective-permute-start.4
  599.1 6.6 collective-permute-start.9
  601.7 9.3 collective-permute-start.5
  605.7 7.9 collective-permute-start.10
  611.0 6.9 collective-permute-start.6
  613.6 11.6 collective-permute-start.11
  625.1 6.5 collective-permute-start.12
  631.7 6.5 collective-permute-start.13
  1157.9 38.5 %copy-start.26 = (f32[128,960]{0,1:T(8,128)S(1)}, f32[128,960]{0,1:T(8,128)}, u32[]{:S(2)}) copy-start(f32[128,960]{0,1:T(8,128)} %get-tuple-element.47) | copy-start | bytes 1474564
  (89 other events, 444.5 us)
Sparse Core Ops, SparseCore 0:
  10.5 30.1 all-gather.75
  42.5 27.3 all-gather.77
  72.4 46.8 all-gather.79
  121.0 42.8 all-gather.81
  166.2 41.1 all-gather.83
  209.7 30.6 all-gather.85
  242.8 27.3 all-gather.87
  272.7 39.7 all-gather.91
  314.9 41.1 all-gather.93
  357.8 39.7 all-gather.89
  422.8 37.3 reduce-scatter.6
  463.3 37.3 reduce-scatter.4
  502.5 27.5 all-gather.49
  531.9 27.6 all-gather.51
  561.8 32.5 all-gather.59
  596.2 31.3 all-gather.57
  631.2 37.3 reduce-scatter.10
  671.6 37.2 reduce-scatter.8
  710.8 27.5 all-gather.45
  740.2 27.6 all-gather.47
  769.7 27.6 all-gather.53
  799.3 27.6 all-gather.55
  828.8 27.6 all-gather.95
  858.8 41.1 all-gather.73
  901.8 27.6 all-gather.71
  931.2 41.1 all-gather.69
  974.6 41.1 all-gather.63
  1017.7 41.1 all-gather.67
  1061.3 41.1 all-gather.61
  1104.2 41.1 all-gather.65
  1151.0 357.5 all-reduce.13
